TPU v7x, 32 devices: a whole 2x2x4 slice. The times are simulated.
32 devices in a mesh: role: 2 (over core), expert: 8 (over z, y), tensor: 2 (over x).
Axes of the slice: x: 2, y: 2, z: 4, core: 2. Of those that a mesh axis runs over, the one named last changes fastest.
Arguments:
- tokens: bfloat16 [512, 2048], P(('role', 'expert'), 'tensor'), may hold values from -180 to 180
- routes: int32 [512, 8], P(('role', 'expert')), may hold values from 0 to 15, all different within a row; in each aligned block of 32 rows (0 to 31, 32 to 63, ...) at most 24 rows name the same one
- gates: float32 [512, 8], P(('role', 'expert')), may hold values from 0.2 to 0.6
- norm_gain: float32 [2048], replicated, may hold values from 0.5 to 2
- w_gate: bfloat16 [16, 768, 2048], P(('role', 'expert'), None, 'tensor'), may hold values from -0.125 to 0.125
- w_up: bfloat16 [16, 768, 2048], P(('role', 'expert'), None, 'tensor'), may hold values from -0.125 to 0.125
- w_down: bfloat16 [16, 768, 2048], P(('role', 'expert'), None, 'tensor'), may hold values from -0.21875 to 0.21875
Outputs:
- moe_out: bfloat16 [512, 2048], P(('role', 'expert'), 'tensor')
Inputs may be any that keep to these rules, and one draw needn't show every extreme that they name: `routes`: each row names 8 different experts. Among the rows of one device (aligned blocks of 32 rows) no expert is named by more than 24 rows, and in every draw some block names some expert exactly 24 times.
All inputs are finite; a program needn't handle non-finite values.
Results may differ from a plain program's by a relative error of at most 0.0072.
Values may be sent and summed in bfloat16 or wider, within the bound.
A program may use at most 64 MiB of HBM per device.

v0:
```python
import jax
import jax.numpy as jnp
from jax import lax
from jax.sharding import PartitionSpec as P


def expert_ffn(arrived, w_gate, w_up, w_down):
    gate = jnp.einsum("sekq,efq->sekf", arrived, w_gate, preferred_element_type=jnp.float32)
    upward = jnp.einsum("sekq,efq->sekf", arrived, w_up, preferred_element_type=jnp.float32)
    gate, upward = lax.psum((gate, upward), "tensor")
    hidden = (jax.nn.silu(gate) * upward).astype(jnp.bfloat16)
    output = jnp.einsum("sekf,efq->sekq", hidden, w_down, preferred_element_type=jnp.float32)
    return output.astype(jnp.bfloat16)


def per_device(tokens, routes, gates, norm_gain, w_gate, w_up, w_down):
    tok_dev, quarter = tokens.shape
    top_k = routes.shape[1]
    exp_dev = w_gate.shape[0]
    n_role = lax.axis_size("role")
    n_expert = lax.axis_size("expert")
    n_tensor = lax.axis_size("tensor")
    devices = n_role * n_expert
    experts = exp_dev * devices
    capacity = min(tok_dev, max(2, 3 * tok_dev * top_k // (2 * experts)))
    width = quarter * n_tensor
    slots = experts * capacity
    picked = routes.reshape(-1)
    one_hot = (picked[:, None] == jnp.arange(experts, dtype=jnp.int32)[None, :]).astype(jnp.int32)
    running = jnp.cumsum(one_hot, axis=0) - one_hot
    earlier = jnp.sum(running * one_hot, axis=1)
    slot_ids = (picked * capacity + earlier).reshape(tok_dev, top_k)
    matches = slot_ids[:, None, :] == jnp.arange(slots, dtype=jnp.int32)[None, :, None]
    pick_rows = jnp.sum(matches.astype(jnp.float32), axis=2).astype(jnp.bfloat16)
    combine = jnp.sum(jnp.where(matches, gates[:, None, :], 0.0), axis=2)
    own = tokens.astype(jnp.float32)
    squares = lax.psum(jnp.sum(own * own, axis=1), "tensor")
    scale = lax.rsqrt(squares / width + 1e-06)[:, None]
    gain_part = lax.dynamic_slice_in_dim(norm_gain, lax.axis_index("tensor") * quarter, quarter)
    normed = (own * scale * gain_part[None, :]).astype(jnp.bfloat16)
    outgoing = jnp.einsum(
        "ts,td->sd", pick_rows, normed, preferred_element_type=jnp.float32
    ).astype(jnp.bfloat16)
    outgoing = outgoing.reshape(devices, exp_dev, capacity, quarter)
    results = expert_ffn(
        lax.all_to_all(outgoing, ("role", "expert"), split_axis=0, concat_axis=0, tiled=True),
        w_gate,
        w_up,
        w_down,
    )
    returned = lax.all_to_all(results, ("role", "expert"), split_axis=0, concat_axis=0, tiled=True)
    returned = returned.reshape(slots, quarter).astype(jnp.float32)
    mixed = jnp.dot(
        combine, returned, precision=lax.Precision.HIGHEST, preferred_element_type=jnp.float32
    )
    return mixed.astype(jnp.bfloat16)


def solution(mesh):
    in_specs = (
        P(("role", "expert"), "tensor"),
        P(("role", "expert"), None),
        P(("role", "expert"), None),
        P(),
        P(("role", "expert"), None, "tensor"),
        P(("role", "expert"), None, "tensor"),
        P(("role", "expert"), None, "tensor"),
    )
    out_specs = P(("role", "expert"), "tensor")
    return jax.shard_map(
        per_device, mesh=mesh, in_specs=in_specs, out_specs=out_specs, check_vma=False
    )
```

profile of v0, /device:TPU:0, one launch (start us, length us, event | category | flops | bytes accessed | tf_op | source)
XLA Modules:
  0.0 154.6 jit_solution(10845132260747476848)
XLA Ops:
  6.5 0.0 copy-start
  6.5 0.0 all-reduce.3.cloned.1.call-start
  6.5 0.9 copy.22
  7.4 0.1 eq.42
  7.5 0.1 eq.38
  7.6 1.0 fusion.21
  8.6 5.8 %psum.21 = f32[32]{0:T(128)S(1)} all-reduce(f32[32]{0:T(128)S(1)} %fusion.21), channel_id=1, replica_groups=mesh['role'=2,'expert'=8,'tensor'=2] {'tensor'}, use_global_device_ids=true, to_apply=%region_6.7 | all-reduce | flops 32 | bytes 256 | tf_op jit(solution)/shard_map/psum | solution.py:37
  14.4 0.6 reduce-window.6
  15.0 0.2 slice_reduce_fusion
  15.2 0.1 fusion.30
  15.3 0.1 reduce_sum.39
  15.4 0.8 copy.26
  16.2 0.7 dynamic_slice.3
  16.9 0.3 convert_reduce_fusion
  17.2 0.0 copy-start.1
  17.2 1.4 convolution_convert_fusion
  18.6 27.9 %all_to_all.10 = bf16[16,1,24,1024]{3,2,1,0:T(8,128)(2,1)S(1)} all-to-all(bf16[16,1,24,1024]{3,2,1,0:T(8,128)(2,1)S(1)} %bitcast.74), channel_id=1, replica_groups=mesh['role'=2,'expert'=8,'tensor'=2] {'role','expert'}, dimensions={0} | all-to-all | bytes 1572864 | tf_op jit(solution)/shard_map/all_to_all | solution.py:46
  46.5 0.0 copy-done.1
  46.5 0.0 copy-start.2
  46.5 1.9 %fusion.12 = f32[16,1,24,768]{3,2,0,1:T(8,128)} fusion(bf16[1,768,1024]{2,1,0:T(8,128)(2,1)S(1)} %copy-done.1, bf16[16,1,24,1024]{3,2,1,0:T(8,128)(2,1)S(1)} %all_to_all.10), kind=kOutput, calls=%fused_computation.9 | convolution fusion | flops 603979776 | bytes 3538944 | tf_op jit(solution)/shard_map/sekq,efq->sekf/dot_general | solution.py:9
  48.3 0.0 copy-done.2
  48.3 1.8 %fusion.9 = f32[16,1,24,768]{3,2,0,1:T(8,128)} fusion(bf16[1,768,1024]{2,1,0:T(8,128)(2,1)S(1)} %copy-done.2, bf16[16,1,24,1024]{3,2,1,0:T(8,128)(2,1)S(1)} %all_to_all.10), kind=kOutput, calls=%fused_computation.8 | convolution fusion | flops 603979776 | bytes 3538944 | tf_op jit(solution)/shard_map/sekq,efq->sekf/dot_general | solution.py:8
  50.2 0.0 all-reduce.3.cloned.1.call-update
  50.2 66.9 %all-reduce.3.cloned.1.call-done = (f32[16,1,24,768]{3,2,0,1:T(8,128)}, f32[16,1,24,768]{3,2,0,1:T(8,128)}) async-done(((f32[16,1,24,768]{3,2,0,1:T(8,128)}, f32[16,1,24,768]{3,2,0,1:T(8,128)}), (f32[16,1,24,768]{3,2,0,1:T(8,128)}, f32[16,1,24,768]{3,2,0,1:T(8,128)})) %all-reduce.3.cloned.1.call-update) | async-done | bytes 2359312 | tf_op jit(solution)/shard_map/psum | solution.py:10
  117.1 0.0 copy-done
  117.1 2.5 %fusion.15 = bf16[16,1,24,1024]{3,2,1,0:T(8,128)(2,1)S(1)} fusion(bf16[1,768,1024]{2,1,0:T(8,128)(2,1)S(1)} %copy-done, f32[16,1,24,768]{3,2,0,1:T(8,128)} %get-tuple-element.7, f32[16,1,24,768]{3,2,0,1:T(8,128)} %get-tuple-element.8), kind=kOutput, calls=%fused_computation.10 | convolution fusion | flops 606142464 | bytes 4718592 | tf_op jit(solution)/shard_map/sekf,efq->sekq/dot_general | solution.py:12
  119.6 27.0 %all_to_all.11 = bf16[16,1,24,1024]{3,2,1,0:T(8,128)(2,1)S(1)} all-to-all(bf16[16,1,24,1024]{3,2,1,0:T(8,128)(2,1)S(1)} %fusion.15), channel_id=1, replica_groups=mesh['role'=2,'expert'=8,'tensor'=2] {'role','expert'}, dimensions={0} | all-to-all | bytes 1572864 | tf_op jit(solution)/shard_map/all_to_all | solution.py:51
  146.6 1.1 convolution_convert_fusion.1
  (5 shorter events, 0.1 us)
Async XLA Ops:
  6.5 110.6 %copy-start = (bf16[1,768,1024]{2,1,0:T(8,128)(2,1)S(1)}, bf16[1,768,1024]{2,1,0:T(8,128)(2,1)}, u32[]{:S(2)}) copy-start(bf16[1,768,1024]{2,1,0:T(8,128)(2,1)} %param.13) | copy-start | bytes 4718596
  6.5 110.6 %all-reduce.3.cloned.1.call-start = ((), (), s32[]{:S(2)}) async-start(), calls=%async_computation.2 | async-start | bytes 4718592 | tf_op jit(solution)/shard_map/psum | solution.py:10
  17.2 29.3 %copy-start.1 = (bf16[1,768,1024]{2,1,0:T(8,128)(2,1)S(1)}, bf16[1,768,1024]{2,1,0:T(8,128)(2,1)}, u32[]{:S(2)}) copy-start(bf16[1,768,1024]{2,1,0:T(8,128)(2,1)} %param.12) | copy-start | bytes 4718596
  46.5 1.9 %copy-start.2 = (bf16[1,768,1024]{2,1,0:T(8,128)(2,1)S(1)}, bf16[1,768,1024]{2,1,0:T(8,128)(2,1)}, u32[]{:S(2)}) copy-start(bf16[1,768,1024]{2,1,0:T(8,128)(2,1)} %param.11) | copy-start | bytes 4718596
Sparse Core Ops, SparseCore 0:
  50.3 66.7 all-reduce.2
where the time goes:
time: 155 us
  waiting for transfers between devices  66.9 us (43%)
  blocking collectives  60.8 us (39%)
  between operations  13.4 us (9%)
  matrix products  8.69 us (6%)
  local copies, waits for them, and re-layouts  2.79 us (2%)
  other arithmetic  2.01 us (1%)
    psum x1, waiting for transfers between devices, expert_ffn(): gate, upward = lax.psum((gate, upward), 'tensor')  66.9 us
    all_to_all x1, blocking collectives, per_device(): lax.all_to_all(outgoing, ('role', 'expert'), split_axis=0, concat_axis=0,...  27.9 us
    all_to_all x1, blocking collectives, per_device(): lax.all_to_all(results, ('role', 'expert'), split_axis=0, concat_axis=0,...  27 us
    psum x1, blocking collectives, per_device(): squares = lax.psum(jnp.sum(own * own, axis=1), 'tensor')  5.84 us
  transfers between devices with their start and end apart: 1, of which 1 were waited for; matrix products, arithmetic and copies ran while one was open for 0% of the time, Pallas kernels for 0%

commit v1 on v0

--- a/solution.py
+++ b/solution.py
@@ -1,7 +1,256 @@
+import functools
+
 import jax
 import jax.numpy as jnp
 from jax import lax
+from jax.experimental import pallas as pl
+from jax.experimental.pallas import tpu as pltpu
 from jax.sharding import PartitionSpec as P
+
+MESH = pl.DeviceIdType.MESH
+F32 = jnp.float32
+BF16 = jnp.bfloat16
+LANES = 128
+
+
+def dot_nt(a, b):
+    return lax.dot_general(a, b, (((1,), (1,)), ((), ())), preferred_element_type=F32)
+
+
+def dot_nn(a, b):
+    return jnp.dot(a, b, preferred_element_type=F32)
+
+
+def moe_kernel(
+    n_expert, top_k, capacity,
+    tokens, routes, gates, gain, wg_hbm, wu_hbm, wd_hbm, out,
+    wg, wu, wd, sq_send, sq_recv, ag, xs, xr, acc, hown, hpeer,
+    cs, cr, ck, ys, yr, yk, zs, zr, fin,
+    w_sem, send_sem, recv_sem,
+):
+    role, expert, tensor = lax.axis_index("role"), lax.axis_index("expert"), lax.axis_index("tensor")
+    nz = n_expert // 2
+    z, y = expert // 2, expert % 2
+    width = tokens.shape[1]
+    tok = tokens.shape[0]
+    experts = 2 * n_expert
+    chunk = 4 * tok
+    rows = 4 * capacity
+    half = wg.shape[0] // 2
+    mine = role * n_expert + expert
+
+    mate = (1 - role, expert, tensor)
+    across = (role, expert, 1 - tensor)
+    ypeer = (role, z * 2 + (1 - y), tensor)
+
+    def zpeer(step):
+        return (role, ((z + step) % nz) * 2 + y, tensor)
+
+    weights = [
+        pltpu.make_async_copy(src, dst, w_sem.at[i])
+        for i, (src, dst) in enumerate(((wg_hbm, wg), (wu_hbm, wu), (wd_hbm, wd)))
+    ]
+    for copy in weights:
+        copy.start()
+
+    barrier = pltpu.get_barrier_semaphore()
+    partners = [across, mate, ypeer] + [zpeer(step) for step in range(1, nz)]
+    for partner in partners:
+        pl.semaphore_signal(barrier, inc=1, device_id=partner, device_id_type=MESH)
+
+    count = [0]
+    pending = []
+
+    def remote(src, dst, device):
+        i = count[0]
+        count[0] += 1
+        copy = pltpu.make_async_remote_copy(
+            src_ref=src, dst_ref=dst, send_sem=send_sem.at[i], recv_sem=recv_sem.at[i],
+            device_id=device, device_id_type=MESH,
+        )
+        copy.start()
+        pending.append(copy)
+        return copy
+
+    own = tokens[...].astype(F32)
+    part = jnp.sum(own * own, axis=1, keepdims=True)
+    sq_send[...] = jnp.broadcast_to(part, (tok, LANES))
+    lane = lax.broadcasted_iota(jnp.int32, (tok, LANES), 1)
+    dense = jnp.zeros((tok, LANES), F32)
+    for k in range(top_k):
+        dense = dense + jnp.where(routes[:, k:k + 1] == lane % experts, gates[:, k:k + 1], 0.0)
+    high = dense.astype(BF16).astype(F32)
+    dense = jnp.where(lane < experts, high, dense - high)
+    ag[0, 0, 0, :, width:] = dense.astype(BF16)
+    pl.semaphore_wait(barrier, len(partners))
+    squares = remote(sq_send, sq_recv, across)
+    gained = gain[:, pl.ds(pl.multiple_of(tensor * width, LANES), width)]
+    squares.wait_recv()
+    total = (part + sq_recv[:, 0:1]) / (2 * width)
+    normed = own * lax.rsqrt(total + 1e-06) * gained
+    ag[0, 0, 0, :, :width] = normed.astype(BF16)
+
+    in_z, in_y, in_c, in_x, in_h, in_cr, in_yr, in_zr = {}, {}, {}, {}, {}, {}, {}, {}
+    picks, scales = {}, {}
+    y_first = remote(ag.at[0, 0, 0], ag.at[0, 0, 1], ypeer)
+    for s in range(1, nz):
+        in_z[s] = remote(ag.at[0, 0, 0], ag.at[s, 0, 0], zpeer(nz - s))
+    in_y[0] = y_first
+    in_c[0, 0] = remote(ag.at[0, 0, 0], ag.at[0, 1, 0], mate)
+
+    def forward_z(s):
+        in_z[s].wait_recv()
+        in_y[s] = remote(ag.at[s, 0, 0], ag.at[s, 0, 1], ypeer)
+        in_c[s, 0] = remote(ag.at[s, 0, 0], ag.at[s, 1, 0], mate)
+
+    def forward_y(s):
+        in_y[s].wait_recv()
+        in_c[s, 1] = remote(ag.at[s, 0, 1], ag.at[s, 1, 1], mate)
+
+    row_id = lax.broadcasted_iota(jnp.int32, (chunk, chunk), 0)
+    col_id = lax.broadcasted_iota(jnp.int32, (chunk, chunk), 1)
+    before = jnp.where(col_id < row_id, 1.0, 0.0).astype(BF16)
+    lane_id = lax.broadcasted_iota(jnp.int32, (chunk, LANES), 1)
+    own_at = pl.ds(pl.multiple_of(tensor * half, LANES), half)
+    peer_at = pl.ds(pl.multiple_of((1 - tensor) * half, LANES), half)
+
+    def project(s):
+        in_c[s, 0].wait_recv()
+        in_c[s, 1].wait_recv()
+        table = ag[s, :, :, :, width:].reshape(chunk, LANES).astype(F32)
+        chosen = (lane_id == mine) | (lane_id == experts + mine)
+        scale = jnp.sum(jnp.where(chosen, table, 0.0), axis=1, keepdims=True)
+        named = jnp.broadcast_to(jnp.where(scale > 0.0, 1.0, 0.0), (chunk, chunk))
+        place = dot_nn(before, named.astype(BF16))
+        pick = jnp.where(place == col_id.astype(F32), named, 0.0)
+        picks[s] = pick.astype(BF16)
+        scales[s] = scale
+        if s == 0:
+            weights[0].wait()
+            weights[1].wait()
+        block = ag[s, :, :, :, :width].reshape(chunk, width)
+        x = dot_nn(pick.T.astype(BF16)[:rows], block).astype(BF16)
+        xs[s, :, :half] = dot_nt(x, wg[peer_at, :]).astype(BF16)
+        xs[s, :, half:] = dot_nt(x, wu[peer_at, :]).astype(BF16)
+        in_x[s] = remote(xs.at[s], xr.at[s], across)
+        acc[s, :, :half] = dot_nt(x, wg[own_at, :])
+        acc[s, :, half:] = dot_nt(x, wu[own_at, :])
+
+    def activate(s):
+        in_x[s].wait_recv()
+        gate = acc[s, :, :half] + xr[s, :, :half].astype(F32)
+        up = acc[s, :, half:] + xr[s, :, half:].astype(F32)
+        hown[s] = (gate / (1.0 + jnp.exp(-gate)) * up).astype(BF16)
+        in_h[s] = remote(hown.at[s], hpeer.at[s], across)
+
+    def descend(s):
+        if s == 0:
+            weights[2].wait()
+        result = dot_nn(hown[s], wd[own_at, :])
+        in_h[s].wait_recv()
+        result = (result + dot_nn(hpeer[s], wd[peer_at, :])).astype(BF16)
+        result = jnp.concatenate([result, jnp.zeros((chunk - rows, width), BF16)], axis=0)
+        share = dot_nn(picks[s], result) * scales[s]
+        cs[s] = share[2 * tok:].astype(BF16)
+        in_cr[s] = remote(cs.at[s], cr.at[s], mate)
+        ck[s] = share[:2 * tok]
+
+    def return_core(s):
+        in_cr[s].wait_recv()
+        ys[s] = (ck[s, tok:] + cr[s, tok:].astype(F32)).astype(BF16)
+        in_yr[s] = remote(ys.at[s], yr.at[s], ypeer)
+        yk[s] = ck[s, :tok] + cr[s, :tok].astype(F32)
+
+    def return_y(s):
+        in_yr[s].wait_recv()
+        value = yk[s] + yr[s].astype(F32)
+        if s == 0:
+            fin[...] = value
+        else:
+            zs[s] = value.astype(BF16)
+            in_zr[s] = remote(zs.at[s], zr.at[s], zpeer(s))
+
+    phases = (
+        (forward_z, 0), (forward_y, 1), (project, 2), (activate, 4),
+        (descend, 6), (return_core, 7), (return_y, 8),
+    )
+    last = max(delay for _, delay in phases) + nz
+    for step in range(last):
+        for phase, delay in phases:
+            s = step - delay
+            if 0 <= s < nz and not (phase is forward_z and s == 0):
+                phase(s)
+
+    value = fin[...]
+    for s in range(1, nz):
+        in_zr[s].wait_recv()
+        value = value + zr[s].astype(F32)
+    out[...] = value.astype(BF16)
+    for copy in pending:
+        copy.wait_send()
+
+
+def gathered(tokens, routes, gates, norm_gain, w_gate, w_up, w_down):
+    tok, width = tokens.shape
+    top_k = routes.shape[1]
+    n_expert = lax.axis_size("expert")
+    experts = 2 * n_expert
+    capacity = min(tok, max(2, 3 * tok * top_k // (2 * experts)))
+    eff = w_gate.shape[1]
+    nz, half, rows = n_expert // 2, eff // 2, 4 * capacity
+    copies = 1 + (nz - 1) + nz + 2 * nz + 4 * nz + (nz - 1)
+    vmem = pl.BlockSpec(memory_space=pltpu.VMEM)
+    hbm = pl.BlockSpec(memory_space=pl.ANY)
+    return pl.pallas_call(
+        functools.partial(moe_kernel, n_expert, top_k, capacity),
+        out_shape=jax.ShapeDtypeStruct((tok, width), BF16),
+        in_specs=[vmem] * 4 + [hbm] * 3,
+        out_specs=vmem,
+        scratch_shapes=[
+            pltpu.VMEM((eff, width), BF16),
+            pltpu.VMEM((eff, width), BF16),
+            pltpu.VMEM((eff, width), BF16),
+            pltpu.VMEM((tok, LANES), F32),
+            pltpu.VMEM((tok, LANES), F32),
+            pltpu.VMEM((nz, 2, 2, tok, width + LANES), BF16),
+            pltpu.VMEM((nz, rows, eff), BF16),
+            pltpu.VMEM((nz, rows, eff), BF16),
+            pltpu.VMEM((nz, rows, eff), F32),
+            pltpu.VMEM((nz, rows, half), BF16),
+            pltpu.VMEM((nz, rows, half), BF16),
+            pltpu.VMEM((nz, 2 * tok, width), BF16),
+            pltpu.VMEM((nz, 2 * tok, width), BF16),
+            pltpu.VMEM((nz, 2 * tok, width), F32),
+            pltpu.VMEM((nz, tok, width), BF16),
+            pltpu.VMEM((nz, tok, width), BF16),
+            pltpu.VMEM((nz, tok, width), F32),
+            pltpu.VMEM((nz, tok, width), BF16),
+            pltpu.VMEM((nz, tok, width), BF16),
+            pltpu.VMEM((tok, width), F32),
+            pltpu.SemaphoreType.DMA((3,)),
+            pltpu.SemaphoreType.DMA((copies,)),
+            pltpu.SemaphoreType.DMA((copies,)),
+        ],
+        compiler_params=pltpu.CompilerParams(
+            collective_id=0, has_side_effects=True, vmem_limit_bytes=40 * 1024 * 1024
+        ),
+    )(
+        tokens, routes, gates, norm_gain.reshape(1, -1),
+        w_gate.reshape(eff, width), w_up.reshape(eff, width), w_down.reshape(eff, width),
+    )
+
+
+def takes_gathered(mesh, tokens, routes, w_gate):
+    sizes = mesh.shape
+    groups = sizes["role"] * sizes["expert"]
+    tok, top_k, experts = tokens.shape[0] // groups, routes.shape[1], w_gate.shape[0]
+    capacity = min(tok, max(2, 3 * tok * top_k // (2 * experts)))
+    return (
+        sizes["role"] == 2 and sizes["tensor"] == 2 and sizes["expert"] % 2 == 0
+        and experts == groups and 2 * top_k >= experts and 2 * experts <= LANES
+        and 4 * tok == LANES and capacity % 4 == 0 and w_gate.shape[1] % (2 * LANES) == 0
+        and tokens.shape[1] % (2 * LANES) == 0
+    )
 
 
 def expert_ffn(arrived, w_gate, w_up, w_down):
@@ -67,6 +316,11 @@
         P(("role", "expert"), None, "tensor"),
     )
     out_specs = P(("role", "expert"), "tensor")
-    return jax.shard_map(
-        per_device, mesh=mesh, in_specs=in_specs, out_specs=out_specs, check_vma=False
-    )
+
+    def layer(tokens, routes, gates, norm_gain, w_gate, w_up, w_down):
+        body = gathered if takes_gathered(mesh, tokens, routes, w_gate) else per_device
+        return jax.shard_map(
+            body, mesh=mesh, in_specs=in_specs, out_specs=out_specs, check_vma=False
+        )(tokens, routes, gates, norm_gain, w_gate, w_up, w_down)
+
+    return layer

time: 155 us -> 56.3 us (0.36)
  waiting for transfers between devices: 66.9 us -> 0 us
  blocking collectives: 60.8 us -> 0 us
  Pallas kernels: 0 us -> 48 us
  between operations: 13.4 us -> 0.02 us
  matrix products: 8.69 us -> 0 us
  local copies, waits for them, and re-layouts: 2.79 us -> 7.91 us
  other arithmetic: 2.01 us -> 0 us
    psum x1 -> x0, waiting for transfers between devices: 66.9 us -> none  [expert_ffn(): gate, upward = lax.psum((gate, upward), 'tensor')]
    all_to_all x2 -> x0, blocking collectives: 54.9 us -> none  [the longest x1 27.9 us: per_device(): lax.all_to_all(outgoing, ('role', 'expert'), split_axis=0, concat_axis=0,...]
    pallas_call x0 -> x1, Pallas kernels: none -> 48 us  [gathered(): pl.pallas_call(functools.partial(moe_kernel, n_expert, top_k, capacity),...]
    dot_general x5 -> x0, matrix products: 8.69 us -> none  [the longest x1 2.51 us: expert_ffn(): jnp.einsum('sekf,efq->sekq', hidden, w_down, preferred_element_type=jnp.f...]
    unnamed x8 -> x13, local copies, waits for them, and re-layouts: 1.66 us -> 7.91 us
    psum x1 -> x0, blocking collectives: 5.84 us -> none  [per_device(): squares = lax.psum(jnp.sum(own * own, axis=1), 'tensor')]
  transfers between devices with their start and end apart: 1 -> 0, of which waited for: 1 -> 0; matrix products, arithmetic and copies ran while one was open for 0% -> 0% of each run, Pallas kernels for 0% -> 0%
where the time goes in v1:
time: 56.3 us; the launch traced here: 55.9 us
  Pallas kernels  48 us (85%)
  local copies, waits for them, and re-layouts  7.91 us (14%)
    pallas_call x1, Pallas kernels, gathered(): pl.pallas_call(functools.partial(moe_kernel, n_expert, top_k, capacity),...  48 us
    unnamed x13, local copies, waits for them, and re-layouts  7.91 us

profile of v1, /device:TPU:0, one launch (start us, length us, event | category | flops | bytes accessed | tf_op | source)
XLA Modules:
  0.0 55.9 jit_solution(6173040248493302218)
XLA Ops:
  0.0 0.8 %copy.8.routes = s32[32,8]{1,0:T(8,128)S(1)} copy(s32[32,8]{0,1:T(8,128)} %param.8) | data formatting | bytes 2048 | tf_op args[1]
  0.8 0.8 %copy.9.gates = f32[32,8]{1,0:T(8,128)S(1)} copy(f32[32,8]{0,1:T(8,128)} %param.9) | data formatting | bytes 2048 | tf_op args[2]
  1.5 0.0 copy-start
  1.5 1.4 %copy-done = bf16[1,768,1024]{2,1,0:T(8,128)(2,1)S(1)} copy-done((bf16[1,768,1024]{2,1,0:T(8,128)(2,1)S(1)}, bf16[1,768,1024]{2,1,0:T(8,128)(2,1)}, u32[]{:S(2)}) %copy-start) | copy-done | bytes 1572888
  2.9 0.0 copy-start.1
  2.9 1.4 %copy-done.1 = bf16[1,768,1024]{2,1,0:T(8,128)(2,1)S(1)} copy-done((bf16[1,768,1024]{2,1,0:T(8,128)(2,1)S(1)}, bf16[1,768,1024]{2,1,0:T(8,128)(2,1)}, u32[]{:S(2)}) %copy-start.1) | copy-done | bytes 1572888
  4.3 0.0 copy-start.2
  4.3 1.4 %copy-done.2 = bf16[1,768,1024]{2,1,0:T(8,128)(2,1)S(1)} copy-done((bf16[1,768,1024]{2,1,0:T(8,128)(2,1)S(1)}, bf16[1,768,1024]{2,1,0:T(8,128)(2,1)}, u32[]{:S(2)}) %copy-start.2) | copy-done | bytes 1572888
  5.7 0.0 copy-start.3
  5.8 0.8 %copy-done.3 = bf16[32,1024]{1,0:T(8,128)(2,1)S(1)} copy-done((bf16[32,1024]{1,0:T(8,128)(2,1)S(1)}, bf16[32,1024]{1,0:T(8,128)(2,1)}, u32[]{:S(2)}) %copy-start.3) | copy-done | bytes 65560
  6.6 0.0 copy-start.4
  6.6 0.7 %copy-done.4 = f32[2048]{0:T(1024)S(1)} copy-done((f32[2048]{0:T(1024)S(1)}, f32[2048]{0:T(1024)}, u32[]{:S(2)}) %copy-start.4) | copy-done | bytes 8216
  7.3 48.0 %shard_map.73 = bf16[32,1024]{1,0:T(8,128)(2,1)S(1)} custom-call(bf16[32,1024]{1,0:T(8,128)(2,1)S(1)} %copy-done.3, s32[32,8]{1,0:T(8,128)S(1)} %copy.8.routes, f32[32,8]{1,0:T(8,128)S(1)} %copy.9.gates, f32[1,2048]{1,0:T(1,128)S(1)} %bitcast.7, bf16[768,1024]{1,0:T(8,128)(2,1)S(1)} %bitcast.4, bf16[768,1024]{1,0:T(8,128)(2,1)S(1)} %bitcast.5, ...), custom_call_target="tpu_custom_call" | custom-call | tf_op jit(solution)/shard_map/pallas_call | solution.py:204
  55.3 0.6 %copy.11 = bf16[32,1024]{1,0:T(8,128)(2,1)} copy(bf16[32,1024]{1,0:T(8,128)(2,1)S(1)} %shard_map.73) | data formatting | bytes 131072
Async XLA Ops:
  1.5 1.4 %copy-start = (bf16[1,768,1024]{2,1,0:T(8,128)(2,1)S(1)}, bf16[1,768,1024]{2,1,0:T(8,128)(2,1)}, u32[]{:S(2)}) copy-start(bf16[1,768,1024]{2,1,0:T(8,128)(2,1)} %param.11) | copy-start | bytes 4718596
  2.9 1.4 %copy-start.1 = (bf16[1,768,1024]{2,1,0:T(8,128)(2,1)S(1)}, bf16[1,768,1024]{2,1,0:T(8,128)(2,1)}, u32[]{:S(2)}) copy-start(bf16[1,768,1024]{2,1,0:T(8,128)(2,1)} %param.12) | copy-start | bytes 4718596
  4.3 1.4 %copy-start.2 = (bf16[1,768,1024]{2,1,0:T(8,128)(2,1)S(1)}, bf16[1,768,1024]{2,1,0:T(8,128)(2,1)}, u32[]{:S(2)}) copy-start(bf16[1,768,1024]{2,1,0:T(8,128)(2,1)} %param.13) | copy-start | bytes 4718596
  5.7 0.8 %copy-start.3 = (bf16[32,1024]{1,0:T(8,128)(2,1)S(1)}, bf16[32,1024]{1,0:T(8,128)(2,1)}, u32[]{:S(2)}) copy-start(bf16[32,1024]{1,0:T(8,128)(2,1)} %tokens.1) | copy-start | bytes 196612
  6.6 0.7 %copy-start.4 = (f32[2048]{0:T(1024)S(1)}, f32[2048]{0:T(1024)}, u32[]{:S(2)}) copy-start(f32[2048]{0:T(1024)} %param.10) | copy-start | bytes 24580

commit v2 on v1

v2 whole, which is shorter than its diff:
```python
import functools

import jax
import jax.numpy as jnp
from jax import lax
from jax.experimental import pallas as pl
from jax.experimental.pallas import tpu as pltpu
from jax.sharding import PartitionSpec as P

MESH = pl.DeviceIdType.MESH
F32 = jnp.float32
BF16 = jnp.bfloat16
LANES = 128
LAG = (1, 2, 3, 4)


def dot_nt(a, b):
    return lax.dot_general(a, b, (((1,), (1,)), ((), ())), preferred_element_type=F32)


def dot_nn(a, b):
    return jnp.dot(a, b, preferred_element_type=F32)


def moe_kernel(
    n_expert, top_k, capacity,
    tokens_hbm, routes_hbm, gates_hbm, gain_hbm, wg_hbm, wu_hbm, wd_hbm, out,
    tokens, routes, gates, gain, wg, wu, wd, sq_send, sq_recv, ag, xs, xr, acc, hown, hpeer,
    cs, cr, ck, ys, yr, yk, zs, zr,
    w_sem, send_sem, recv_sem,
):
    role, expert, tensor = lax.axis_index("role"), lax.axis_index("expert"), lax.axis_index("tensor")
    nz = n_expert // 2
    z, y = expert // 2, expert % 2
    tok, width = tokens.shape
    experts = 2 * n_expert
    half = wg.shape[0] // 2
    mine = role * n_expert + expert

    mate = (1 - role, expert, tensor)
    across = (role, expert, 1 - tensor)
    ypeer = (role, z * 2 + (1 - y), tensor)

    def zpeer(step):
        return (role, ((z + step) % nz) * 2 + y, tensor)

    barrier = pltpu.get_barrier_semaphore()
    partners = [across, mate, ypeer] + [zpeer(step) for step in range(1, nz)]
    for partner in partners:
        pl.semaphore_signal(barrier, inc=1, device_id=partner, device_id_type=MESH)

    gain_part = gain_hbm.at[:, pl.ds(pl.multiple_of(tensor * width, LANES), width)]
    loads = [
        pltpu.make_async_copy(src, dst, w_sem.at[i])
        for i, (src, dst) in enumerate((
            (tokens_hbm, tokens), (routes_hbm, routes), (gates_hbm, gates), (gain_part, gain),
            (wg_hbm, wg), (wu_hbm, wu), (wd_hbm, wd),
        ))
    ]
    for copy in loads:
        copy.start()

    count = [0]
    pending = []

    def remote(src, dst, device):
        i = count[0]
        count[0] += 1
        copy = pltpu.make_async_remote_copy(
            src_ref=src, dst_ref=dst, send_sem=send_sem.at[i], recv_sem=recv_sem.at[i],
            device_id=device, device_id_type=MESH,
        )
        copy.start()
        pending.append(copy)
        return copy

    loads[0].wait()
    own = tokens[...].astype(F32)
    part = jnp.sum(own * own, axis=1, keepdims=True)
    sq_send[...] = jnp.broadcast_to(part, (tok, LANES))
    pl.semaphore_wait(barrier, len(partners))
    squares = remote(sq_send, sq_recv, across)

    loads[1].wait()
    loads[2].wait()
    loads[3].wait()
    entry = lax.broadcasted_iota(jnp.int32, (LANES, tok), 0)
    dense = jnp.zeros((LANES, tok), F32)
    for k in range(top_k):
        dense = dense + jnp.where(routes[k:k + 1, :] == entry % experts, gates[k:k + 1, :], 0.0)
    high = dense.astype(BF16).astype(F32)
    dense = jnp.where(entry < experts, high, dense - high)
    ag[0, 0, 0, :, width:] = dense.T.astype(BF16)
    gained = gain[...]
    squares.wait_recv()
    total = (part + sq_recv[:, 0:1]) / (2 * width)
    normed = own * lax.rsqrt(total + 1e-06) * gained
    ag[0, 0, 0, :, :width] = normed.astype(BF16)

    in_z, in_y, in_c, in_x, in_h, in_cr, in_yr, in_zr = {}, {}, {}, {}, {}, {}, {}, {}
    picks, scales = {}, {}
    in_y[0] = remote(ag.at[0, 0, 0], ag.at[0, 1, 0], ypeer)
    near = sorted(range(1, nz), key=lambda s: min(s, nz - s))
    waves = [[s for s in near if min(s, nz - s) == d] for d in range(1, nz // 2 + 1)]

    def send_wave(number):
        if number:
            for s in waves[number - 1]:
                in_z[s].wait_send()
                pending[:] = [copy for copy in pending if copy is not in_z[s]]
        for s in waves[number]:
            in_z[s] = remote(ag.at[0, 0, 0], ag.at[s, 0, 0], zpeer(nz - s))

    if waves:
        send_wave(0)
    in_c[0, 0] = remote(ag.at[0, 0, 0], ag.at[0, 0, 1], mate)

    def forward_z(s):
        in_z[s].wait_recv()
        in_y[s] = remote(ag.at[s, 0, 0], ag.at[s, 1, 0], ypeer)
        in_c[s, 0] = remote(ag.at[s, 0, 0], ag.at[s, 0, 1], mate)

    def forward_y(s):
        in_y[s].wait_recv()
        in_c[s, 1] = remote(ag.at[s, 1, 0], ag.at[s, 1, 1], mate)

    own_at = pl.ds(pl.multiple_of(tensor * half, LANES), half)
    peer_at = pl.ds(pl.multiple_of((1 - tensor) * half, LANES), half)
    groups = [(0, 0, 1), (0, 1, 1)] + [(s, 0, 2) for s in near]

    def project(g):
        s, first, many = groups[g]
        at = pl.ds(first, many)
        for i in range(first, first + many):
            in_c[s, i].wait_recv()
        chunk, rows = many * 2 * tok, many * 2 * capacity
        table = ag[s, at, :, :, width:].reshape(chunk, LANES).astype(F32)
        lane = lax.broadcasted_iota(jnp.int32, (chunk, LANES), 1)
        chosen = (lane == mine) | (lane == experts + mine)
        scale = jnp.sum(jnp.where(chosen, table, 0.0), axis=1, keepdims=True)
        named = jnp.broadcast_to(jnp.where(scale > 0.0, 1.0, 0.0), (chunk, LANES))
        row_id = lax.broadcasted_iota(jnp.int32, (chunk, chunk), 0)
        col_id = lax.broadcasted_iota(jnp.int32, (chunk, chunk), 1)
        before = jnp.where(col_id < row_id, 1.0, 0.0).astype(BF16)
        place = dot_nn(before, named.astype(BF16))
        pick = jnp.where(place == lane.astype(F32), named, 0.0)
        picks[g] = pick.astype(BF16)
        scales[g] = scale
        if g == 0:
            loads[4].wait()
            loads[5].wait()
        block = ag[s, at, :, :, :width].reshape(chunk, width)
        x = dot_nn(pick.T.astype(BF16)[:rows], block).astype(BF16)
        shape = (many, 2 * capacity, half)
        xs[s, at, :, :half] = dot_nt(x, wg[peer_at, :]).astype(BF16).reshape(shape)
        xs[s, at, :, half:] = dot_nt(x, wu[peer_at, :]).astype(BF16).reshape(shape)
        in_x[g] = remote(xs.at[s, at], xr.at[s, at], across)
        acc[s, at, :, :half] = dot_nt(x, wg[own_at, :]).reshape(shape)
        acc[s, at, :, half:] = dot_nt(x, wu[own_at, :]).reshape(shape)

    def activate(g):
        s, first, many = groups[g]
        at = pl.ds(first, many)
        in_x[g].wait_recv()
        gate = acc[s, at, :, :half] + xr[s, at, :, :half].astype(F32)
        up = acc[s, at, :, half:] + xr[s, at, :, half:].astype(F32)
        hown[s, at] = (gate / (1.0 + jnp.exp(-gate)) * up).astype(BF16)
        in_h[g] = remote(hown.at[s, at], hpeer.at[s, at], across)

    def descend(g):
        s, first, many = groups[g]
        at = pl.ds(first, many)
        rows = many * 2 * capacity
        if g == 0:
            loads[6].wait()
        result = dot_nn(hown[s, at].reshape(rows, half), wd[own_at, :])
        in_h[g].wait_recv()
        result = (result + dot_nn(hpeer[s, at].reshape(rows, half), wd[peer_at, :])).astype(BF16)
        result = jnp.concatenate([result, jnp.zeros((LANES - rows, width), BF16)], axis=0)
        share = (dot_nn(picks[g], result) * scales[g]).reshape(many, 2, tok, width)
        cs[s, at] = share[:, 1].astype(BF16)
        in_cr[g] = remote(cs.at[s, at], cr.at[s, at], mate)
        ck[s, at] = share[:, 0]

    def return_core(g):
        s, first, many = groups[g]
        in_cr[g].wait_recv()
        for i in reversed(range(first, first + many)):
            value = ck[s, i] + cr[s, i].astype(F32)
            if i == 1:
                ys[s] = value.astype(BF16)
                in_yr[s] = remote(ys.at[s], yr.at[s], ypeer)
            else:
                yk[s] = value

    def return_y(s):
        in_yr[s].wait_recv()
        zs[s] = (yk[s] + yr[s].astype(F32)).astype(BF16)
        in_zr[s] = remote(zs.at[s], zr.at[s], zpeer(s))

    n = len(groups)

    def ready_z(g):
        if g < n and groups[g][0] and groups[g][1] == 0:
            forward_z(groups[g][0])

    def ready_y(g):
        if g < n and sum(groups[g][1:]) == 2:
            forward_y(groups[g][0])

    def finish(g):
        if groups[g][0]:
            return_y(groups[g][0])

    ready_z(0)
    ready_y(0)
    for step in range(n + LAG[3]):
        if step < n:
            project(step)
            if step + 1 < len(waves):
                send_wave(step + 1)
            if step == 0:
                ready_z(1)
            ready_z(step + 2)
            ready_y(step + 1)
        for phase, delay in zip((activate, descend, return_core, finish), LAG):
            if 0 <= step - delay < n:
                phase(step - delay)

    value = yk[0]
    in_yr[0].wait_recv()
    value = value + yr[0].astype(F32)
    for s in range(1, nz):
        in_zr[s].wait_recv()
        value = value + zr[s].astype(F32)
    out[...] = value.astype(BF16)
    for copy in pending:
        copy.wait_send()


def gathered(tokens, routes, gates, norm_gain, w_gate, w_up, w_down):
    tok, width = tokens.shape
    top_k = routes.shape[1]
    n_expert = lax.axis_size("expert")
    experts = 2 * n_expert
    capacity = min(tok, max(2, 3 * tok * top_k // (2 * experts)))
    eff = w_gate.shape[1]
    nz, half, rows = n_expert // 2, eff // 2, 2 * capacity
    copies = 1 + (nz - 1) + nz + 2 * nz + 3 * (nz + 1) + nz + (nz - 1)
    vmem = pl.BlockSpec(memory_space=pltpu.VMEM)
    hbm = pl.BlockSpec(memory_space=pl.ANY)
    return pl.pallas_call(
        functools.partial(moe_kernel, n_expert, top_k, capacity),
        out_shape=jax.ShapeDtypeStruct((tok, width), BF16),
        in_specs=[hbm] * 7,
        out_specs=vmem,
        scratch_shapes=[
            pltpu.VMEM((tok, width), BF16),
            pltpu.VMEM((top_k, tok), jnp.int32),
            pltpu.VMEM((top_k, tok), F32),
            pltpu.VMEM((1, width), F32),
            pltpu.VMEM((eff, width), BF16),
            pltpu.VMEM((eff, width), BF16),
            pltpu.VMEM((eff, width), BF16),
            pltpu.VMEM((tok, LANES), F32),
            pltpu.VMEM((tok, LANES), F32),
            pltpu.VMEM((nz, 2, 2, tok, width + LANES), BF16),
            pltpu.VMEM((nz, 2, rows, eff), BF16),
            pltpu.VMEM((nz, 2, rows, eff), BF16),
            pltpu.VMEM((nz, 2, rows, eff), F32),
            pltpu.VMEM((nz, 2, rows, half), BF16),
            pltpu.VMEM((nz, 2, rows, half), BF16),
            pltpu.VMEM((nz, 2, tok, width), BF16),
            pltpu.VMEM((nz, 2, tok, width), BF16),
            pltpu.VMEM((nz, 2, tok, width), F32),
            pltpu.VMEM((nz, tok, width), BF16),
            pltpu.VMEM((nz, tok, width), BF16),
            pltpu.VMEM((nz, tok, width), F32),
            pltpu.VMEM((nz, tok, width), BF16),
            pltpu.VMEM((nz, tok, width), BF16),
            pltpu.SemaphoreType.DMA((7,)),
            pltpu.SemaphoreType.DMA((copies,)),
            pltpu.SemaphoreType.DMA((copies,)),
        ],
        compiler_params=pltpu.CompilerParams(
            collective_id=0, has_side_effects=True, vmem_limit_bytes=63 * 1024 * 1024
        ),
    )(
        tokens, routes.T, gates.T, norm_gain.reshape(1, -1),
        w_gate.reshape(eff, width), w_up.reshape(eff, width), w_down.reshape(eff, width),
    )


def takes_gathered(mesh, tokens, routes, w_gate):
    sizes = mesh.shape
    groups = sizes["role"] * sizes["expert"]
    tok, top_k, experts = tokens.shape[0] // groups, routes.shape[1], w_gate.shape[0]
    capacity = min(tok, max(2, 3 * tok * top_k // (2 * experts)))
    return (
        sizes["role"] == 2 and sizes["tensor"] == 2 and sizes["expert"] % 2 == 0
        and experts == groups and 2 * top_k >= experts and 2 * experts <= LANES
        and 4 * tok == LANES and capacity % 4 == 0 and w_gate.shape[1] % (2 * LANES) == 0
        and tokens.shape[1] % (2 * LANES) == 0
    )


def expert_ffn(arrived, w_gate, w_up, w_down):
    gate = jnp.einsum("sekq,efq->sekf", arrived, w_gate, preferred_element_type=jnp.float32)
    upward = jnp.einsum("sekq,efq->sekf", arrived, w_up, preferred_element_type=jnp.float32)
    gate, upward = lax.psum((gate, upward), "tensor")
    hidden = (jax.nn.silu(gate) * upward).astype(jnp.bfloat16)
    output = jnp.einsum("sekf,efq->sekq", hidden, w_down, preferred_element_type=jnp.float32)
    return output.astype(jnp.bfloat16)


def per_device(tokens, routes, gates, norm_gain, w_gate, w_up, w_down):
    tok_dev, quarter = tokens.shape
    top_k = routes.shape[1]
    exp_dev = w_gate.shape[0]
    n_role = lax.axis_size("role")
    n_expert = lax.axis_size("expert")
    n_tensor = lax.axis_size("tensor")
    devices = n_role * n_expert
    experts = exp_dev * devices
    capacity = min(tok_dev, max(2, 3 * tok_dev * top_k // (2 * experts)))
    width = quarter * n_tensor
    slots = experts * capacity
    picked = routes.reshape(-1)
    one_hot = (picked[:, None] == jnp.arange(experts, dtype=jnp.int32)[None, :]).astype(jnp.int32)
    running = jnp.cumsum(one_hot, axis=0) - one_hot
    earlier = jnp.sum(running * one_hot, axis=1)
    slot_ids = (picked * capacity + earlier).reshape(tok_dev, top_k)
    matches = slot_ids[:, None, :] == jnp.arange(slots, dtype=jnp.int32)[None, :, None]
    pick_rows = jnp.sum(matches.astype(jnp.float32), axis=2).astype(jnp.bfloat16)
    combine = jnp.sum(jnp.where(matches, gates[:, None, :], 0.0), axis=2)
    own = tokens.astype(jnp.float32)
    squares = lax.psum(jnp.sum(own * own, axis=1), "tensor")
    scale = lax.rsqrt(squares / width + 1e-06)[:, None]
    gain_part = lax.dynamic_slice_in_dim(norm_gain, lax.axis_index("tensor") * quarter, quarter)
    normed = (own * scale * gain_part[None, :]).astype(jnp.bfloat16)
    outgoing = jnp.einsum(
        "ts,td->sd", pick_rows, normed, preferred_element_type=jnp.float32
    ).astype(jnp.bfloat16)
    outgoing = outgoing.reshape(devices, exp_dev, capacity, quarter)
    results = expert_ffn(
        lax.all_to_all(outgoing, ("role", "expert"), split_axis=0, concat_axis=0, tiled=True),
        w_gate,
        w_up,
        w_down,
    )
    returned = lax.all_to_all(results, ("role", "expert"), split_axis=0, concat_axis=0, tiled=True)
    returned = returned.reshape(slots, quarter).astype(jnp.float32)
    mixed = jnp.dot(
        combine, returned, precision=lax.Precision.HIGHEST, preferred_element_type=jnp.float32
    )
    return mixed.astype(jnp.bfloat16)


def solution(mesh):
    in_specs = (
        P(("role", "expert"), "tensor"),
        P(("role", "expert"), None),
        P(("role", "expert"), None),
        P(),
        P(("role", "expert"), None, "tensor"),
        P(("role", "expert"), None, "tensor"),
        P(("role", "expert"), None, "tensor"),
    )
    out_specs = P(("role", "expert"), "tensor")

    def layer(tokens, routes, gates, norm_gain, w_gate, w_up, w_down):
        body = gathered if takes_gathered(mesh, tokens, routes, w_gate) else per_device
        return jax.shard_map(
            body, mesh=mesh, in_specs=in_specs, out_specs=out_specs, check_vma=False
        )(tokens, routes, gates, norm_gain, w_gate, w_up, w_down)

    return layer
```

time: 56.3 us -> 46.7 us (0.83)
  local copies, waits for them, and re-layouts: 7.91 us -> 1.47 us
  Pallas kernels: 48 us -> 45 us
    unnamed x13 -> x1, local copies, waits for them, and re-layouts: 7.91 us -> 1.47 us
    pallas_call x1, Pallas kernels: 48 us -> 45 us  [gathered(): pl.pallas_call(functools.partial(moe_kernel, n_expert, top_k, capacity),...]
where the time goes in v2:
time: 46.7 us; the launch traced here: 46.5 us
  Pallas kernels  45 us (96%)
  local copies, waits for them, and re-layouts  1.47 us (3%)
    pallas_call x1, Pallas kernels, gathered(): pl.pallas_call(functools.partial(moe_kernel, n_expert, top_k, capacity),...  45 us
    unnamed x1, local copies, waits for them, and re-layouts  1.47 us

profile of v2, /device:TPU:0, one launch (start us, length us, event | category | flops | bytes accessed | tf_op | source)
XLA Modules:
  0.0 46.5 jit_solution(11835441687775589256)
XLA Ops:
  0.0 45.0 %shard_map.73 = bf16[32,1024]{1,0:T(8,128)(2,1)} custom-call(bf16[32,1024]{1,0:T(8,128)(2,1)} %tokens_hbm.1, s32[8,32]{1,0:T(8,128)} %bitcast.10, f32[8,32]{1,0:T(8,128)} %bitcast.11, f32[1,2048]{1,0:T(1,128)} %bitcast.9, bf16[768,1024]{1,0:T(8,128)(2,1)} %bitcast.6, bf16[768,1024]{1,0:T(8,128)(2,1)} %bitcast.7, bf16[768,1024]{1,0:T(8,128)(2,1)} %bitcast.8), custom_call_target="tpu_custom_call" | custom-call | tf_op jit(solution)/shard_map/pallas_call | solution.py:252
  45.0 1.5 %copy.9 = bf16[32,1024]{1,0:T(8,128)(2,1)} copy(bf16[32,1024]{1,0:T(8,128)(2,1)} %shard_map.73) | data formatting | bytes 131072

commit v3 on v2

--- a/solution.py
+++ b/solution.py
@@ -99,6 +99,7 @@
 
     in_z, in_y, in_c, in_x, in_h, in_cr, in_yr, in_zr = {}, {}, {}, {}, {}, {}, {}, {}
     picks, scales = {}, {}
+    in_c[0, 0] = remote(ag.at[0, 0, 0], ag.at[0, 0, 1], mate)
     in_y[0] = remote(ag.at[0, 0, 0], ag.at[0, 1, 0], ypeer)
     near = sorted(range(1, nz), key=lambda s: min(s, nz - s))
     waves = [[s for s in near if min(s, nz - s) == d] for d in range(1, nz // 2 + 1)]
@@ -113,7 +114,6 @@
 
     if waves:
         send_wave(0)
-    in_c[0, 0] = remote(ag.at[0, 0, 0], ag.at[0, 0, 1], mate)
 
     def forward_z(s):
         in_z[s].wait_recv()

time: 46.7 us -> 46.7 us (level)
  no operation moved by 1% of the time
where the time goes in v3:
time: 46.7 us; the launch traced here: 46.5 us
  Pallas kernels  45 us (96%)
  local copies, waits for them, and re-layouts  1.47 us (3%)
    pallas_call x1, Pallas kernels, gathered(): pl.pallas_call(functools.partial(moe_kernel, n_expert, top_k, capacity),...  45 us
    unnamed x1, local copies, waits for them, and re-layouts  1.47 us

profile of v3, /device:TPU:0, one launch (start us, length us, event | category | flops | bytes accessed | tf_op | source)
XLA Modules:
  0.0 46.5 jit_solution(8910089590885512177)
XLA Ops:
  0.0 45.0 %shard_map.73 = bf16[32,1024]{1,0:T(8,128)(2,1)} custom-call(bf16[32,1024]{1,0:T(8,128)(2,1)} %tokens_hbm.1, s32[8,32]{1,0:T(8,128)} %bitcast.10, f32[8,32]{1,0:T(8,128)} %bitcast.11, f32[1,2048]{1,0:T(1,128)} %bitcast.9, bf16[768,1024]{1,0:T(8,128)(2,1)} %bitcast.6, bf16[768,1024]{1,0:T(8,128)(2,1)} %bitcast.7, bf16[768,1024]{1,0:T(8,128)(2,1)} %bitcast.8), custom_call_target="tpu_custom_call" | custom-call | tf_op jit(solution)/shard_map/pallas_call | solution.py:252
  45.0 1.5 %copy.9 = bf16[32,1024]{1,0:T(8,128)(2,1)} copy(bf16[32,1024]{1,0:T(8,128)(2,1)} %shard_map.73) | data formatting | bytes 131072
